TPU v7x, 32 devices: a whole 2x2x4 slice. The times are simulated.
32 devices in a mesh: seq: 8 (over z, core), wsh: 4 (over y, x).
Axes of the slice: x: 2, y: 2, z: 4, core: 2. Of those that a mesh axis runs over, the one named last changes fastest.
Arguments:
- x_in: bfloat16 [4, 8192, 1024], P('wsh', 'seq'), may hold values from -6 to 6
- seg_ids: int32 [4, 8192], P('wsh'), may hold values from 0 to 11, as said below
- g_norm: float32 [1024], replicated, may hold values from 0.25 to 1.75
- w_in: bfloat16 [1024, 4384], P('wsh'), may hold values from -0.1875 to 0.1875
- conv_w: float32 [4, 2304], replicated, may hold values from -3 to 3
- conv_b: float32 [2304], replicated, may hold values from -3 to 3
- dt_bias: float32 [32], replicated, may hold values from -9 to -2
- a_log: float32 [32], replicated, may hold values from 0 to 2.77
- d_skip: float32 [32], replicated, may hold values from 0.5 to 2
- g_gate: float32 [2048], replicated, may hold values from 0.25 to 1.75
- w_out: bfloat16 [2048, 1024], P('wsh'), may hold values from -0.125 to 0.125
- cotangent: bfloat16 [4, 8192, 1024], P('wsh', 'seq'), may hold values from -6 to 6
Outputs:
- out: bfloat16 [4, 8192, 1024], P('wsh', 'seq')
- x_grad: float32 [4, 8192, 1024], P('wsh', 'seq')
- g_norm_grad: float32 [1024], replicated
- w_in_grad: float32 [1024, 4384], P('wsh')
- conv_w_grad: float32 [4, 2304], replicated
- conv_b_grad: float32 [2304], replicated
- dt_bias_grad: float32 [32], replicated
- a_log_grad: float32 [32], replicated
- d_skip_grad: float32 [32], replicated
- g_gate_grad: float32 [2048], replicated
- w_out_grad: float32 [2048, 1024], P('wsh')
Inputs may be any that keep to these rules, and one draw needn't show every extreme that they name: `seg_ids`: in group g (first dimension) the ids along the 8192 positions are 3g, then 3g+1, then 3g+2, each present; id 3g+1 starts within the first 1024 positions and ends within the last 1024.
All inputs are finite; a program needn't handle non-finite values.
Results may differ from a plain program's by a relative error of at most 0.012.
Values may be sent and summed in bfloat16 or wider, within the bound.
No kernel may reach another device: no remote copies, remote signals or barrier semaphores. Data moves between devices by JAX's collectives and lax.ppermute only.
A program may use at most 320 MiB of HBM per device.

v0:
```python
from functools import partial

import jax
import jax.numpy as jnp
from jax import lax
from jax.sharding import PartitionSpec as P

STATE = 128
STRETCH = 256


EPSILON = 1e-05
EXACT = lax.Precision.HIGHEST


def causal_conv(values, kernel, offset_bias, segment):
    length = values.shape[0]
    taps = kernel.shape[0]
    conv_total = jnp.zeros_like(values) + offset_bias[None, :]
    for offset in range(taps):
        moved_rows = jnp.concatenate(
            [jnp.zeros((offset, values.shape[1]), values.dtype), values[: length - offset]], axis=0
        )
        moved_segment = jnp.concatenate(
            [jnp.full((offset,), -1, jnp.int32), segment[: length - offset]], axis=0
        )
        keeping = (moved_segment == segment).astype(values.dtype)
        conv_total = conv_total + kernel[taps - 1 - offset][None, :] * moved_rows * keeping[:, None]
    return conv_total


def stretch_step(carried, pieces, decay_rates):
    state_now, previous = carried
    values, b_rows, c_rows, step_sizes, segment = pieces
    block_width = values.shape[0]
    log_steps = step_sizes * decay_rates[None, :]
    cumulative = jnp.cumsum(log_steps, axis=0)
    later_pos = lax.broadcasted_iota(jnp.int32, (block_width, block_width), 0)
    earlier_pos = lax.broadcasted_iota(jnp.int32, (block_width, block_width), 1)
    linked = (segment[:, None] == segment[None, :]) & (later_pos >= earlier_pos)
    spread_log = cumulative.T[:, :, None] - cumulative.T[:, None, :]
    decay_table = jnp.where(linked[None], jnp.exp(jnp.where(linked[None], spread_log, 0.0)), 0.0)
    intersection = jnp.dot(c_rows, b_rows.T, precision=EXACT)
    mixing = decay_table * intersection[None] * step_sizes.T[:, None, :]
    inside = jnp.einsum("hts,shp->thp", mixing, values, precision=EXACT)
    entering = jnp.exp(cumulative) * (segment == previous).astype(values.dtype)[:, None]
    outside = jnp.einsum("tn,hpn->thp", c_rows, state_now, precision=EXACT) * entering[:, :, None]
    last_segment = segment[-1]
    leaving = (
        jnp.exp(cumulative[-1][None, :] - cumulative)
        * step_sizes
        * (segment == last_segment).astype(values.dtype)[:, None]
    )
    fresh_state = jnp.einsum("sh,shp,sn->hpn", leaving, values, b_rows, precision=EXACT)
    keep_state = (last_segment == previous).astype(values.dtype)
    state_now = state_now * (jnp.exp(cumulative[-1]) * keep_state)[:, None, None] + fresh_state
    return ((state_now, last_segment), inside + outside)


def state_scan(values, b_rows, c_rows, step_sizes, decay_rates, segment):
    length, head_count, head_width = values.shape
    stretch_count = length // STRETCH
    pieces = (
        values.reshape(stretch_count, STRETCH, head_count, head_width),
        b_rows.reshape(stretch_count, STRETCH, b_rows.shape[1]),
        c_rows.reshape(stretch_count, STRETCH, c_rows.shape[1]),
        step_sizes.reshape(stretch_count, STRETCH, head_count),
        segment.reshape(stretch_count, STRETCH),
    )
    initial = (jnp.zeros((head_count, head_width, b_rows.shape[1]), values.dtype), jnp.int32(-1))
    stepper = jax.checkpoint(lambda carried, piece: stretch_step(carried, piece, decay_rates))
    final_carry, outputs = lax.scan(stepper, initial, pieces)
    return outputs.reshape(length, head_count, head_width)


def local_mixer(
    gate_in,
    x_heads,
    step_raw,
    bc_in,
    conv_w,
    conv_b,
    dt_bias,
    a_log,
    d_skip,
    segment,
    channel_start,
    head_start,
):
    block_width = x_heads.shape[1]
    head_count = step_raw.shape[1]
    inner = conv_w.shape[1] - 2 * STATE
    kernel = jnp.concatenate(
        [lax.dynamic_slice_in_dim(conv_w, channel_start, block_width, 1), conv_w[:, inner:]], axis=1
    )
    offset_bias = jnp.concatenate(
        [lax.dynamic_slice_in_dim(conv_b, channel_start, block_width, 0), conv_b[inner:]], axis=0
    )
    mixed = jax.nn.silu(
        causal_conv(jnp.concatenate([x_heads, bc_in], axis=1), kernel, offset_bias, segment)
    )
    length = mixed.shape[0]
    values = mixed[:, :block_width].reshape(length, head_count, block_width // head_count)
    b_rows = mixed[:, block_width : block_width + STATE]
    c_rows = mixed[:, block_width + STATE :]
    step_sizes = jax.nn.softplus(
        step_raw + lax.dynamic_slice_in_dim(dt_bias, head_start, head_count, 0)[None, :]
    )
    decay_rates = -jnp.exp(lax.dynamic_slice_in_dim(a_log, head_start, head_count, 0))
    skip_gain = lax.dynamic_slice_in_dim(d_skip, head_start, head_count, 0)
    result = (
        state_scan(values, b_rows, c_rows, step_sizes, decay_rates, segment)
        + skip_gain[None, :, None] * values
    )
    return result.reshape(length, block_width) * jax.nn.silu(gate_in)


def on_device(
    x_in, seg_ids, g_norm, w_in, conv_w, conv_b, dt_bias, a_log, d_skip, g_gate, w_out, cotangent
):
    seq_count = lax.axis_size("seq")
    my_index = lax.axis_index("seq")
    inner = g_gate.shape[0]
    head_total = dt_bias.shape[0]
    my_heads = head_total // seq_count
    my_width = inner // seq_count
    channel_start = my_index * my_width
    head_start = my_index * my_heads
    segment = seg_ids[0]
    tok_rows = x_in[0].astype(jnp.float32)
    root_scale = lax.rsqrt(jnp.mean(tok_rows * tok_rows, axis=1, keepdims=True) + EPSILON)
    normed = (tok_rows * root_scale * g_norm[None, :]).astype(jnp.bfloat16)
    in_full, out_full = (
        lax.all_gather(w_in, "wsh", axis=0, tiled=True),
        lax.all_gather(w_out, "wsh", axis=0, tiled=True),
    )
    projected = jnp.dot(normed, in_full, preferred_element_type=jnp.float32).astype(jnp.bfloat16)
    gate_tok = projected[:, :inner]
    x_tok = projected[:, inner : 2 * inner]
    bc_tok = projected[:, 2 * inner : 2 * inner + 2 * STATE]
    step_tok = projected[:, 2 * inner + 2 * STATE :]
    gate_heads, x_heads, step_heads = (
        lax.all_to_all(gate_tok, "seq", split_axis=1, concat_axis=0, tiled=True),
        lax.all_to_all(x_tok, "seq", split_axis=1, concat_axis=0, tiled=True),
        lax.all_to_all(step_tok, "seq", split_axis=1, concat_axis=0, tiled=True),
    )
    bc_whole = lax.all_gather(bc_tok, "seq", axis=0, tiled=True)
    mixer_fn = partial(
        local_mixer, segment=segment, channel_start=channel_start, head_start=head_start
    )
    gated, mixer_back = jax.vjp(
        mixer_fn,
        gate_heads.astype(jnp.float32),
        x_heads.astype(jnp.float32),
        step_heads.astype(jnp.float32),
        bc_whole.astype(jnp.float32),
        conv_w,
        conv_b,
        dt_bias,
        a_log,
        d_skip,
    )
    square_sums = lax.psum(jnp.sum(gated * gated, axis=1), "seq")
    gate_scale = lax.rsqrt(square_sums / inner + EPSILON)
    gain_part = lax.dynamic_slice_in_dim(g_gate, channel_start, my_width, 0)
    normed_heads = (gated * gate_scale[:, None] * gain_part[None, :]).astype(jnp.bfloat16)
    normed_tok = lax.all_to_all(normed_heads, "seq", split_axis=0, concat_axis=1, tiled=True)
    branch_out = jnp.dot(normed_tok, out_full, preferred_element_type=jnp.float32)
    result = (tok_rows + branch_out).astype(jnp.bfloat16)
    cot_rows = cotangent[0]
    grad_norm_tok = jnp.dot(cot_rows, out_full.T, preferred_element_type=jnp.float32).astype(
        jnp.bfloat16
    )
    grad_heads = lax.all_to_all(
        grad_norm_tok, "seq", split_axis=1, concat_axis=0, tiled=True
    ).astype(jnp.float32)
    weighted = grad_heads * gain_part[None, :]
    cross_sums = lax.psum(jnp.sum(gated * weighted, axis=1), "seq")
    grad_gated = (
        gate_scale[:, None] * weighted
        - gated * (gate_scale * gate_scale * gate_scale * cross_sums / inner)[:, None]
    )
    gain_grad_part = jnp.sum(grad_heads * gated * gate_scale[:, None], axis=0)
    grads_local = mixer_back(grad_gated)
    grad_gate_tok, grad_x_tok, grad_step_tok = (
        lax.all_to_all(
            grads_local[0].astype(jnp.bfloat16), "seq", split_axis=0, concat_axis=1, tiled=True
        ),
        lax.all_to_all(
            grads_local[1].astype(jnp.bfloat16), "seq", split_axis=0, concat_axis=1, tiled=True
        ),
        lax.all_to_all(
            grads_local[2].astype(jnp.bfloat16), "seq", split_axis=0, concat_axis=1, tiled=True
        ),
    )
    grad_bc_tok = lax.psum_scatter(
        grads_local[3].astype(jnp.bfloat16), "seq", scatter_dimension=0, tiled=True
    )
    grad_proj = jnp.concatenate([grad_gate_tok, grad_x_tok, grad_bc_tok, grad_step_tok], axis=1)
    grad_normed = jnp.dot(grad_proj, in_full.T, preferred_element_type=jnp.float32)
    scaled_grad = grad_normed * g_norm[None, :]
    mean_cross = jnp.mean(scaled_grad * tok_rows, axis=1, keepdims=True)
    x_grad = (
        cot_rows.astype(jnp.float32)
        + root_scale * scaled_grad
        - tok_rows * root_scale * root_scale * root_scale * mean_cross
    )
    g_norm_part = jnp.sum(grad_normed * tok_rows * root_scale, axis=0)
    in_term = jnp.dot(normed.T, grad_proj, preferred_element_type=jnp.float32)
    out_term = jnp.dot(normed_tok.T, cot_rows, preferred_element_type=jnp.float32)
    in_rows, out_rows = (
        lax.psum_scatter(in_term, "wsh", scatter_dimension=0, tiled=True),
        lax.psum_scatter(out_term, "wsh", scatter_dimension=0, tiled=True),
    )
    w_in_grad, w_out_grad = lax.psum((in_rows, out_rows), "seq")
    gate_gain_grad = lax.dynamic_update_slice_in_dim(
        jnp.zeros_like(g_gate), gain_grad_part, channel_start, 0
    )
    summed_small = lax.psum(
        (
            g_norm_part,
            grads_local[4],
            grads_local[5],
            grads_local[6],
            grads_local[7],
            grads_local[8],
            gate_gain_grad,
        ),
        ("seq", "wsh"),
    )
    return (
        result[None],
        x_grad[None],
        summed_small[0],
        w_in_grad,
        summed_small[1],
        summed_small[2],
        summed_small[3],
        summed_small[4],
        summed_small[5],
        summed_small[6],
        w_out_grad,
    )


def solution(mesh):
    return jax.shard_map(
        on_device,
        mesh=mesh,
        in_specs=(
            P("wsh", "seq", None),
            P("wsh", None),
            P(),
            P("wsh", None),
            P(),
            P(),
            P(),
            P(),
            P(),
            P(),
            P("wsh", None),
            P("wsh", "seq", None),
        ),
        out_specs=(
            P("wsh", "seq", None),
            P("wsh", "seq", None),
            P(),
            P("wsh", None),
            P(),
            P(),
            P(),
            P(),
            P(),
            P(),
            P("wsh", None),
        ),
        check_vma=False,
    )
```

profile of v0, /device:TPU:0, one launch (start us, length us, event | category | flops | bytes accessed | tf_op | source)
XLA Modules:
  0.0 3137.3 jit_solution(17838638106170252750)
XLA Ops:
  10.8 94.2 %all-gather.4.cloned.1.call-done = bf16[1024,4384]{0,1:T(8,128)(2,1)} async-done(((bf16[256,4384]{0,1:T(8,128)(2,1)}), bf16[1024,4384]{0,1:T(8,128)(2,1)}) %all-gather.4.cloned.1.call-update) | async-done | bytes 8978448 | tf_op jit(solution)/shard_map/all_gather | solution.py:134
  105.0 12.9 convolution_convert_fusion
  126.6 32.9 %all-gather.8.cloned.1.call-done = bf16[2048,1024]{1,0:T(8,128)(2,1)} async-done(((bf16[512,1024]{1,0:T(8,128)(2,1)}), bf16[2048,1024]{1,0:T(8,128)(2,1)}) %all-gather.8.cloned.1.call-update) | async-done | bytes 4194320 | tf_op jit(solution)/shard_map/all_gather | solution.py:135
  159.5 8.3 convolution_convert_fusion.1
  184.9 88.1 %all-to-all-done.4 = bf16[1024,8,256]{0,2,1:T(8,128)(2,1)} async-done(((bf16[1024,8,256]{0,2,1:T(8,128)(2,1)}), bf16[1024,8,256]{0,2,1:T(8,128)(2,1)}, u32[]{:S(2)}, u32[]{:S(2)}) %all-to-all-start.4) | async-done | bytes 4194336 | tf_op jit(solution)/shard_map/all_to_all | solution.py:174
  291.3 114.0 %all-to-all-done.1 = bf16[1024,8,256]{0,2,1:T(8,128)(2,1)} async-done(((bf16[1024,8,256]{0,2,1:T(8,128)(2,1)}), bf16[1024,8,256]{0,2,1:T(8,128)(2,1)}, u32[]{:S(2)}, u32[]{:S(2)}) %all-to-all-start.1) | async-done | bytes 4194336 | tf_op jit(solution)/shard_map/all_to_all | solution.py:144
  415.1 11.4 maximum_convert_fusion
  426.5 36.4 %fusion.87 = (f32[8192,512]{0,1:T(8,128)}, f32[8192,512]{0,1:T(8,128)}) fusion(f32[8192]{0:T(1024)S(1)} %get-tuple-element.915, f32[8189,512]{0,1:T(8,128)} %bitcast.476, f32[512]{0:T(512)S(1)} %bitcast.542, f32[8192]{0:T(1024)S(1)} %get-tuple-element.916, f32[8190,512]{0,1:T(8,128)} %bitcast.477, f32[512]{0:T(512)S(1)} %bitcast.546, ...), kind=kLoop, calls=%fused_computation.154 | loop fusion | flops 79691776 | bytes 92370944 | tf_op jit(solution)/shard_map/jvp(jit(silu))/mul | solution.py:99
  462.9 8.7 slice.193
  484.8 8.1 copy.227
  508.4 612.3 %while.46 = (s32[]{:T(128)}, f32[4,64,128]{2,1,0:T(8,128)S(1)}, s32[]{:T(128)}, f32[32,256,4,64]{1,0,3,2:T(8,128)}, f32[32,4,64,128]{3,2,1,0:T(8,128)}, /*index=...) while((s32[]{:T(128)}, f32[4,64,128]{2,1,0:T(8,128)S(1)}, ...), condition=%wide.region_4.5_spmd.clone, body=%wide.region_1.4_spmd.clone.sunk | while | flops 505321504 | bytes 4292835 | solution.py:72
  1120.8 14.3 copy.297
  1146.4 10.3 multiply_reduce_fusion.11
  1156.7 29.5 psum.77
  1186.2 8.0 multiply_reduce_fusion.8
  1194.2 25.9 psum.78
  1220.1 20.0 multiply_reduce_fusion.9
  1256.1 1023.8 %while.47 = (s32[]{:T(128)}, f32[4]{0:T(128)S(1)}, f32[4,64,128]{2,1,0:T(8,128)S(1)}, f32[32,256,4,64]{1,0,3,2:T(8,128)}, f32[32,256,128]{2,1,0:T(8,128)}, /*ind...) while((s32[]{:T(128)}, f32[4]{0:T(128)S(1)}, ...), condition=%wide.region_22.23_spmd.clone, body=%wide.region_9.22_spmd.clone.sunk | while | flops 1214437376 | bytes 11291974 | solution.py:72
  1792.2 7.0 dynamic_update_slice.114
  1824.2 7.0 dynamic_update_slice.114
  1888.2 7.0 dynamic_update_slice.114
  1984.1 7.0 dynamic_update_slice.114
  2048.1 7.1 dynamic_update_slice.114
  2080.1 7.1 dynamic_update_slice.114
  2112.1 7.1 dynamic_update_slice.114
  2144.1 7.1 dynamic_update_slice.114
  2176.1 7.1 dynamic_update_slice.114
  2208.1 7.1 dynamic_update_slice.114
  2240.1 7.1 dynamic_update_slice.114
  2272.1 7.1 dynamic_update_slice.114
  2279.9 14.4 copy.299
  2294.3 11.2 multiply_add_fusion.1
  2316.8 27.5 multiply_reduce_fusion.7
  2344.4 30.8 multiply_reduce_fusion.6
  2375.2 14.7 slice_multiply_fusion.1
  2391.6 9.6 slice_multiply_fusion
  2402.5 7.6 slice_multiply_fusion.2
  2410.2 27.1 fusion.141
  2454.4 125.0 %all-to-all-done.3 = bf16[8,1024,256]{1,2,0:T(8,128)(2,1)} async-done(((bf16[8,1024,256]{1,2,0:T(8,128)(2,1)}), bf16[8,1024,256]{1,2,0:T(8,128)(2,1)}, u32[]{:S(2)}, u32[]{:S(2)}) %all-to-all-start.3) | async-done | bytes 4194336 | tf_op jit(solution)/shard_map/all_to_all | solution.py:167
  2582.8 9.1 fusion.105
  2606.8 89.0 %all-to-all-done.6 = bf16[8,1024,256]{1,2,0:T(8,128)(2,1)} async-done(((bf16[8,1024,256]{1,2,0:T(8,128)(2,1)}), bf16[8,1024,256]{1,2,0:T(8,128)(2,1)}, u32[]{:S(2)}, u32[]{:S(2)}) %all-to-all-start.6) | async-done | bytes 4194336 | tf_op jit(solution)/shard_map/all_to_all | solution.py:189
  2700.4 93.9 %all-to-all-done.5 = bf16[8,1024,256]{1,2,0:T(8,128)(2,1)} async-done(((bf16[8,1024,256]{1,2,0:T(8,128)(2,1)}), bf16[8,1024,256]{1,2,0:T(8,128)(2,1)}, u32[]{:S(2)}, u32[]{:S(2)}) %all-to-all-start.5) | async-done | bytes 4194336 | tf_op jit(solution)/shard_map/all_to_all | solution.py:186
  2794.4 21.4 fusion.108
  2818.3 9.9 fusion.104
  2828.2 149.9 %reduce-scatter.6.cloned.1.call-done = f32[256,4384]{0,1:T(8,128)} async-done(((f32[1024,4384]{0,1:T(8,128)}), f32[256,4384]{0,1:T(8,128)}) %reduce-scatter.6.cloned.1.call-update) | async-done | bytes 4489232 | tf_op jit(solution)/shard_map/reduce_scatter | solution.py:212
  2978.2 16.8 fusion.103
  2995.0 42.2 %all-reduce.19 = (f32[1024]{0:T(1024)}, f32[4,2304]{1,0:T(4,128)}, f32[2304]{0:T(1024)}, f32[32]{0:T(128)}, f32[32]{0:T(128)}, /*index=5*/f32[32]{0:T(128)}, f32[2048]{0:T(1024)}) all-reduce(f32[1024]{0:T(1024)S(1)} %get-tuple-element.798, f32[4,2304]{1,0:T(4,128)S(1)} %fusion.132, ...), channel_id=1, replica_groups=mesh['seq'=8,'wsh'=4] {'seq','wsh'}, use_global_device_ids=true, to_apply=%region_26.27 | all-reduce | flops 14688 | bytes 117504 | tf_op jit(solution)/shard_map/psum | solution.py:219
  3042.1 82.0 %all-reduce.23.cloned.1.call-done = (f32[256,4384]{0,1:T(8,128)}, f32[512,1024]{1,0:T(8,128)}) async-done(((f32[256,4384]{0,1:T(8,128)}, f32[512,1024]{1,0:T(8,128)}), (f32[256,4384]{0,1:T(8,128)}, f32[512,1024]{1,0:T(8,128)})) %all-reduce.23.cloned.1.call-update) | async-done | bytes 6586384 | tf_op jit(solution)/shard_map/psum | solution.py:215
  (2652 shorter events, 1641.9 us)
Async XLA Ops:
  7.2 97.8 %all-gather.4.cloned.1.call-start = ((), (), s32[]{:S(2)}) async-start(), calls=%async_computation.11 | async-start | bytes 11223040 | tf_op jit(solution)/shard_map/all_gather | solution.py:134
  7.9 151.6 %all-gather.8.cloned.1.call-start = ((), (), s32[]{:S(2)}) async-start(), calls=%async_computation.13 | async-start | bytes 5242880 | tf_op jit(solution)/shard_map/all_gather | solution.py:135
  10.7 94.2 %copy-start.29 = (f32[1024]{0:T(1024)}, f32[1024]{0:T(1024)S(1)}, u32[]{:S(2)}) copy-start(f32[1024]{0:T(1024)S(1)} %add_rsqrt_fusion.1) | copy-start | bytes 12292
  10.8 148.8 %copy-start.7 = (bf16[1,1024,1024]{2,1,0:T(8,128)(2,1)S(1)}, bf16[1,1024,1024]{2,1,0:T(8,128)(2,1)}, u32[]{:S(2)}) copy-start(bf16[1,1024,1024]{2,1,0:T(8,128)(2,1)} %param.27) | copy-start | bytes 6291460
  122.0 52.2 %all-to-all-start = ((bf16[1024,8,4]{0,2,1:T(4,128)(2,1)}), bf16[1024,8,4]{0,2,1:T(4,128)(2,1)S(1)}, u32[]{:S(2)}, u32[]{:S(2)}) async-start(bf16[1024,8,4]{0,2,1:T(4,128)(2,1)} %all_to_all.94), calls=%async_computation | async-start | bytes 131072 | tf_op jit(solution)/shard_map/all_to_all | solution.py:145
  174.2 109.5 %copy-start.13 = (bf16[1024,8,4]{0,2,1:T(4,128)(2,1)}, bf16[1024,8,4]{0,2,1:T(4,128)(2,1)S(1)}, u32[]{:S(2)}) copy-start(bf16[1024,8,4]{0,2,1:T(4,128)(2,1)S(1)} %all-to-all-done) | copy-start | bytes 196612
  174.2 98.7 %all-to-all-start.4 = ((bf16[1024,8,256]{0,2,1:T(8,128)(2,1)}), bf16[1024,8,256]{0,2,1:T(8,128)(2,1)}, u32[]{:S(2)}, u32[]{:S(2)}) async-start(bf16[1024,8,256]{0,2,1:T(8,128)(2,1)} %bitcast.504), calls=%async_computation.4 | async-start | bytes 8388608 | tf_op jit(solution)/shard_map/all_to_all | solution.py:174
  184.9 95.2 %copy-start.12 = (s32[1,8192]{1,0:T(1,128)S(1)}, s32[1,8192]{1,0:T(1,128)}, u32[]{:S(2)}) copy-start(s32[1,8192]{1,0:T(1,128)} %param.17) | copy-start | bytes 98308
  184.9 95.9 %copy-start.39 = (f32[32]{0:T(128)S(1)}, f32[32]{0:T(128)}, u32[]{:S(2)}) copy-start(f32[32]{0:T(128)} %param.22) | copy-start | bytes 388
  184.9 96.0 %copy-start.40 = (f32[32]{0:T(128)S(1)}, f32[32]{0:T(128)}, u32[]{:S(2)}) copy-start(f32[32]{0:T(128)} %param.24) | copy-start | bytes 388
  184.9 97.0 %copy-start.36 = (f32[32]{0:T(128)S(1)}, f32[32]{0:T(128)}, u32[]{:S(2)}) copy-start(f32[32]{0:T(128)} %param.23) | copy-start | bytes 388
  273.0 132.3 %all-to-all-start.1 = ((bf16[1024,8,256]{0,2,1:T(8,128)(2,1)}), bf16[1024,8,256]{0,2,1:T(8,128)(2,1)}, u32[]{:S(2)}, u32[]{:S(2)}) async-start(bf16[1024,8,256]{0,2,1:T(8,128)(2,1)} %bitcast.508), calls=%async_computation.1 | async-start | bytes 8388608 | tf_op jit(solution)/shard_map/all_to_all | solution.py:144
  277.5 137.5 %all-gather.6.cloned.1.call-start = ((), (), s32[]{:S(2)}) async-start(), calls=%async_computation.12 | async-start | bytes 4718592 | tf_op jit(solution)/shard_map/all_gather | solution.py:147
  280.9 10.4 copy-start.31
  283.6 142.9 %copy-start.19 = (f32[1,512]{1,0:T(1,128)}, f32[1,512]{1,0:T(1,128)S(1)}, u32[]{:S(2)}) copy-start(f32[1,512]{1,0:T(1,128)S(1)} %get-tuple-element.919) | copy-start | bytes 6148
  283.6 142.9 %copy-start.21 = (f32[1,512]{1,0:T(1,128)}, f32[1,512]{1,0:T(1,128)S(1)}, u32[]{:S(2)}) copy-start(f32[1,512]{1,0:T(1,128)S(1)} %get-tuple-element.921) | copy-start | bytes 6148
  283.6 142.9 %copy-start.23 = (f32[1,512]{1,0:T(1,128)}, f32[1,512]{1,0:T(1,128)S(1)}, u32[]{:S(2)}) copy-start(f32[1,512]{1,0:T(1,128)S(1)} %get-tuple-element.920) | copy-start | bytes 6148
  283.6 142.9 %copy-start.25 = (f32[1,512]{1,0:T(1,128)}, f32[1,512]{1,0:T(1,128)S(1)}, u32[]{:S(2)}) copy-start(f32[1,512]{1,0:T(1,128)S(1)} %get-tuple-element.922) | copy-start | bytes 6148
  283.7 142.8 %copy-start.15 = (f32[8192]{0:T(1024)}, f32[8192]{0:T(1024)S(1)}, u32[]{:S(2)}) copy-start(f32[8192]{0:T(1024)S(1)} %get-tuple-element.914) | copy-start | bytes 98308
  283.7 142.8 %copy-start.17 = (f32[8192]{0:T(1024)}, f32[8192]{0:T(1024)S(1)}, u32[]{:S(2)}) copy-start(f32[8192]{0:T(1024)S(1)} %get-tuple-element.916) | copy-start | bytes 98308
  405.2 729.9 %all-to-all-start.2 = ((bf16[1024,8,256]{0,2,1:T(8,128)(2,1)}), bf16[1024,8,256]{0,2,1:T(8,128)(2,1)}, u32[]{:S(2)}, u32[]{:S(2)}) async-start(bf16[1024,8,256]{0,2,1:T(8,128)(2,1)} %bitcast.507), calls=%async_computation.2 | async-start | bytes 8388608 | tf_op jit(solution)/shard_map/all_to_all | solution.py:143
  409.8 2384.6 %reduce-scatter.4.cloned.1.call-start = ((), (), s32[]{:S(2)}) async-start(), calls=%async_computation.14 | async-start | bytes 4718592 | tf_op jit(solution)/shard_map/reduce_scatter | solution.py:196
  462.9 11.2 copy-start
  1135.1 11.1 slice-start
  1146.2 10.4 copy-start.2
  2279.9 14.5 copy-start.27
  2316.8 27.6 copy-start.16
  2316.8 27.6 copy-start.18
  2344.3 30.8 copy-start.26
  2375.1 16.4 copy-start.4
  2375.1 16.4 copy-start.24
  2375.1 26.0 slice-start.2
  2375.2 26.0 slice-start.3
  2391.6 11.0 slice-start.5
  2391.6 11.0 copy-start.22
  2443.4 10.0 copy-start.14
  2443.4 139.4 %copy-start.8 = (bf16[1,1024,1024]{2,1,0:T(8,128)(2,1)S(1)}, bf16[1,1024,1024]{2,1,0:T(8,128)(2,1)}, u32[]{:S(2)}) copy-start(bf16[1,1024,1024]{2,1,0:T(8,128)(2,1)} %param.27) | copy-start | bytes 6291460
  2448.4 131.0 %all-to-all-start.3 = ((bf16[8,1024,256]{1,2,0:T(8,128)(2,1)}), bf16[8,1024,256]{1,2,0:T(8,128)(2,1)}, u32[]{:S(2)}, u32[]{:S(2)}) async-start(bf16[8,1024,256]{1,2,0:T(8,128)(2,1)} %bitcast.506), calls=%async_computation.3 | async-start | bytes 8388608 | tf_op jit(solution)/shard_map/all_to_all | solution.py:167
  2579.4 17.3 all-to-all-start.7
  2582.7 245.5 %reduce-scatter.8.cloned.1.call-start = ((), (), s32[]{:S(2)}) async-start(), calls=%async_computation.16 | async-start | bytes 10485760 | tf_op jit(solution)/shard_map/reduce_scatter | solution.py:213
  2596.7 99.1 %all-to-all-start.6 = ((bf16[8,1024,256]{1,2,0:T(8,128)(2,1)}), bf16[8,1024,256]{1,2,0:T(8,128)(2,1)}, u32[]{:S(2)}, u32[]{:S(2)}) async-start(bf16[8,1024,256]{1,2,0:T(8,128)(2,1)} %bitcast.505), calls=%async_computation.6 | async-start | bytes 8388608 | tf_op jit(solution)/shard_map/all_to_all | solution.py:189
  2601.7 192.7 %copy-start.6 = (bf16[1,1024,1024]{2,1,0:T(8,128)(2,1)S(1)}, bf16[1,1024,1024]{2,1,0:T(8,128)(2,1)}, u32[]{:S(2)}) copy-start(bf16[1,1024,1024]{2,1,0:T(8,128)(2,1)} %param.16) | copy-start | bytes 6291460
  2601.7 192.7 %copy-start.30 = (f32[1024]{0:T(1024)S(1)}, f32[1024]{0:T(1024)}, u32[]{:S(2)}) copy-start(f32[1024]{0:T(1024)} %copy-done.29) | copy-start | bytes 12292
  2601.7 192.7 %copy-start.33 = (f32[1024]{0:T(1024)S(1)}, f32[1024]{0:T(1024)}, u32[]{:S(2)}) copy-start(f32[1024]{0:T(1024)} %param.18) | copy-start | bytes 12292
  2695.8 98.6 %all-to-all-start.5 = ((bf16[8,1024,256]{1,2,0:T(8,128)(2,1)}), bf16[8,1024,256]{1,2,0:T(8,128)(2,1)}, u32[]{:S(2)}, u32[]{:S(2)}) async-start(bf16[8,1024,256]{1,2,0:T(8,128)(2,1)} %bitcast.503), calls=%async_computation.5 | async-start | bytes 8388608 | tf_op jit(solution)/shard_map/all_to_all | solution.py:186
  2700.4 277.8 %reduce-scatter.6.cloned.1.call-start = ((), (), s32[]{:S(2)}) async-start(), calls=%async_computation.15 | async-start | bytes 22446080 | tf_op jit(solution)/shard_map/reduce_scatter | solution.py:212
  2815.8 308.3 %all-reduce.23.cloned.1.call-start = ((), (), s32[]{:S(2)}) async-start(), calls=%async_computation.17 | async-start | bytes 13172736 | tf_op jit(solution)/shard_map/psum | solution.py:215
  2818.3 159.9 %copy-start.38 = (bf16[1024,256]{0,1:T(8,128)(2,1)S(1)}, bf16[1024,256]{0,1:T(8,128)(2,1)}, u32[]{:S(2)}) copy-start(bf16[1024,256]{0,1:T(8,128)(2,1)} %reduce-scatter.4.cloned.1.call-done) | copy-start | bytes 1572868
  (14 other events, 69.9 us)
Sparse Core Ops, SparseCore 0:
  9.8 95.0 all-gather.3
  106.8 52.7 all-gather.7
  280.6 80.7 all-gather.5
  2443.5 93.6 reduce-scatter.3
  2592.0 87.6 reduce-scatter.7
  2815.9 162.1 reduce-scatter.5
  2980.6 143.4 all-reduce.22
where the time goes:
time: 3170 us; the launch traced here: 3140 us
  local copies, waits for them, and re-layouts  885 us (28%)
  waiting for transfers between devices  871 us (27%)
  other arithmetic  607 us (19%)
  matrix products  535 us (17%)
  blocking collectives  97.7 us (3%)
  loops' own time  90.6 us (3%)
  starting transfers between devices  37 us (1%)
    dynamic_update_slice x160, local copies, waits for them, and re-layouts, state_scan(): final_carry, outputs = lax.scan(stepper, initial, pieces)  470 us
    another operation x256, other arithmetic  247 us
    dot_general x96, matrix products, stretch_step(): inside = jnp.einsum('hts,shp->thp', mixing, values, precision=EXACT)  167 us
    reduce_scatter x1, waiting for transfers between devices, on_device(): lax.psum_scatter(in_term, 'wsh', scatter_dimension=0, tiled=True)  150 us
    dot_general x128, matrix products, stretch_step(): intersection = jnp.dot(c_rows, b_rows.T, precision=EXACT)  128 us
    all_to_all x1, waiting for transfers between devices, on_device(): lax.all_to_all(normed_heads, 'seq', split_axis=0, concat_axis=1, tiled=True)  125 us
    all_to_all x1, waiting for transfers between devices, on_device(): lax.all_to_all(x_tok, 'seq', split_axis=1, concat_axis=0, tiled=True)  114 us
    all_gather x1, waiting for transfers between devices, on_device(): lax.all_gather(w_in, 'wsh', axis=0, tiled=True)  94.2 us
  transfers between devices with their start and end apart: 15, of which 9 were waited for; matrix products, arithmetic and copies ran while one was open for 26% of the time, Pallas kernels for 0%

commit v1 on v0

v1 whole, which is shorter than its diff:
```python
from functools import partial

import jax
import jax.numpy as jnp
from jax import lax
from jax.experimental import pallas as pl
from jax.experimental.pallas import tpu as pltpu
from jax.sharding import PartitionSpec as P

STATE = 128
CHUNK = 128
HALO = 16
EPSILON = 1e-05
EXACT = lax.Precision.HIGHEST
BF = jnp.bfloat16
F32 = jnp.float32
VMEM_LIMIT = 56 * 1024 * 1024


def dot(a, b):
    return jnp.dot(a, b, preferred_element_type=F32)


def dot_tt(a, b):
    return lax.dot_general(a, b, (((1,), (1,)), ((), ())), preferred_element_type=F32)


def dot_00(a, b):
    return lax.dot_general(a, b, (((0,), (0,)), ((), ())), preferred_element_type=F32)


def sigmoid(v):
    return 1.0 / (1.0 + jnp.exp(-v))


def params():
    return pltpu.CompilerParams(vmem_limit_bytes=VMEM_LIMIT, dimension_semantics=("arbitrary",))


def conv_kernel(x_ref, keep_ref, w_ref, b_ref, z_ref, buf):
    rows = z_ref.shape[0]
    buf[...] = x_ref[...].astype(F32)
    taps = w_ref.shape[0]
    for start in range(0, rows, CHUNK):
        keep = keep_ref[start : start + CHUNK, :]
        total = b_ref[...] + w_ref[taps - 1 : taps, :] * buf[HALO + start : HALO + start + CHUNK, :]
        for k in range(1, taps):
            moved = buf[HALO + start - k : HALO + start - k + CHUNK, :]
            total = total + w_ref[taps - 1 - k : taps - k, :] * (moved * keep[:, k : k + 1])
        z_ref[start : start + CHUNK, :] = total.astype(BF)


def conv_back_kernel(dz_ref, x_ref, keep_ref, next_ref, w_ref, dx_ref, dw_ref, db_ref, buf, dbuf):
    rows, width = dz_ref.shape
    taps = w_ref.shape[0]
    buf[...] = x_ref[...].astype(F32)
    dbuf[0:HALO, :] = jnp.zeros((HALO, width), F32)
    dbuf[HALO : HALO + rows, :] = dz_ref[...].astype(F32)
    dbuf[HALO + rows :, :] = jnp.zeros((8, width), F32)
    sums = [jnp.zeros((1, width), F32) for _ in range(taps + 1)]
    for start in range(0, rows, CHUNK):
        keep = keep_ref[start : start + CHUNK, :]
        dz = dbuf[HALO + start : HALO + start + CHUNK, :]
        sums[taps] = sums[taps] + jnp.sum(dz, axis=0, keepdims=True)
        for k in range(taps):
            moved = buf[HALO + start - k : HALO + start - k + CHUNK, :]
            if k:
                moved = moved * keep[:, k : k + 1]
            sums[k] = sums[k] + jnp.sum(dz * moved, axis=0, keepdims=True)
    for k in range(taps):
        dw_ref[taps - 1 - k : taps - k, :] = sums[k]
    db_ref[...] = sums[taps]
    for start in range(0, rows + HALO, HALO * 13):
        count = min(HALO * 13, rows + HALO - start)
        total = w_ref[taps - 1 : taps, :] * dbuf[start : start + count, :]
        nxt = next_ref[start : start + count, :]
        for k in range(1, taps):
            moved = dbuf[start + k : start + k + count, :]
            total = total + w_ref[taps - 1 - k : taps - k, :] * (moved * nxt[:, k : k + 1])
        dx_ref[start : start + count, :] = total.astype(BF)


def state_kernel(z_ref, tok_ref, spread_ref, s_ref):
    inner = s_ref.shape[1]

    @pl.when(pl.program_id(0) == 0)
    def _():
        s_ref[...] = jnp.zeros_like(s_ref)

    z = z_ref[:, : inner + STATE].astype(F32)
    mixed = z * sigmoid(z)
    factor = dot(tok_ref[...].astype(BF), spread_ref[...])
    s_ref[...] += dot_00(mixed[:, inner:].astype(BF), (mixed[:, :inner] * factor).astype(BF))


def decay_pair(tok, cum_rows, head, heads):
    gap = tok[:, heads + head : heads + head + 1] - cum_rows[head : head + 1, :]
    return jnp.exp(jnp.minimum(gap, 0.0))


def linked_mask(seg_col, seg_row):
    later = lax.broadcasted_iota(jnp.int32, (CHUNK, CHUNK), 0)
    earlier = lax.broadcasted_iota(jnp.int32, (CHUNK, CHUNK), 1)
    return (seg_col == seg_row) & (later >= earlier)


def two_heads(pair):
    lane = lax.broadcasted_iota(jnp.int32, pair.shape, 1)
    zero = jnp.zeros_like(pair)
    half = pair.shape[1] // 2
    return jnp.where(lane < half, pair, zero), jnp.where(lane >= half, pair, zero)


def inside_kernel(heads, z_ref, tok_ref, seg_ref, cum_ref, segrow_ref, spread_ref, skip_ref, y_ref):
    inner = y_ref.shape[1]
    pair_width = 2 * inner // heads
    z = z_ref[...].astype(F32)
    mixed = z * sigmoid(z)
    tok = tok_ref[...]
    xc = mixed[:, :inner]
    xt = (xc * dot(tok.astype(BF), spread_ref[...])).astype(BF)
    b_rows = mixed[:, inner : inner + STATE].astype(BF)
    c_rows = mixed[:, inner + STATE :].astype(BF)
    mask = linked_mask(seg_ref[...], segrow_ref[...])
    cross = jnp.where(mask, dot_tt(c_rows, b_rows), 0.0)
    cum_rows = cum_ref[...]
    for j in range(heads // 2):
        at = slice(j * pair_width, (j + 1) * pair_width)
        left = [(cross * decay_pair(tok, cum_rows, 2 * j + i, heads)).astype(BF) for i in (0, 1)]
        right = two_heads(xt[:, at])
        part = dot(jnp.concatenate(left, axis=1), jnp.concatenate(right, axis=0))
        y_ref[:, at] = (part + skip_ref[:, at] * xc[:, at]).astype(BF)


def gate_kernel(
    yi_ref, z_ref, gate_ref, back_ref, tok_ref, far_ref, decay_ref, gain_ref, s0_ref,
    spread_ref, spread_ent_ref, spread_leave_ref,
    sin_ref, out_ref, dgate_ref, dy_ref, dgain_ref, dskip_ref, ds_ref, state,
):
    inner = yi_ref.shape[1]

    @pl.when(pl.program_id(0) == 0)
    def _():
        state[...] = s0_ref[...]
        dgain_ref[...] = jnp.zeros_like(dgain_ref)
        dskip_ref[...] = jnp.zeros_like(dskip_ref)
        ds_ref[...] = jnp.zeros_like(ds_ref)

    z = z_ref[...].astype(F32)
    mixed = z * sigmoid(z)
    xc = mixed[:, :inner]
    b_rows = mixed[:, inner : inner + STATE].astype(BF)
    c_rows = mixed[:, inner + STATE :].astype(BF)
    tok = tok_ref[...].astype(BF)
    now = state[...]
    now_bf = now.astype(BF)
    sin_ref[0] = now_bf
    y = yi_ref[...].astype(F32) + dot(c_rows, now_bf) * dot(tok, spread_ent_ref[...])
    leave = (xc * dot(tok, spread_ref[...])) * dot(tok, spread_leave_ref[...])
    state[...] = now * decay_ref[0] + dot_00(b_rows, leave.astype(BF))
    gate = gate_ref[...].astype(F32)
    sg = sigmoid(gate)
    silu = gate * sg
    v = y * silu
    gain = gain_ref[...]
    q = lax.rsqrt(jnp.mean(v * v, axis=1, keepdims=True) + EPSILON)
    vq = v * q
    out_ref[...] = (vq * gain).astype(BF)
    back = back_ref[...].astype(F32)
    e = back * gain
    cross = jnp.mean(vq * e, axis=1, keepdims=True)
    dv = q * (e - vq * cross)
    dgain_ref[...] += jnp.sum(back * vq, axis=0, keepdims=True)
    dgate_ref[...] = (dv * y * (sg * (1.0 + gate * (1.0 - sg)))).astype(BF)
    dy = dv * silu
    dy_ref[...] = dy.astype(BF)
    dskip_ref[...] += jnp.sum(dy * xc, axis=0, keepdims=True)
    ds_ref[...] += dot_00(c_rows, (dy * dot(far_ref[...].astype(BF), spread_ent_ref[...])).astype(BF))


def back_kernel(
    heads, dy_ref, z_ref, tok_ref, seg_ref, cum_ref, segrow_ref, decay_ref, skip_ref, sin_ref, ds0_ref,
    spread_ref, spread_ent_ref, spread_leave_ref, gather_ref,
    dz_ref, tokg_ref, inlog_ref, carry_ref, dstate, dxt,
):
    inner = dy_ref.shape[1]
    pair_width = 2 * inner // heads

    @pl.when(pl.program_id(0) == 0)
    def _():
        dstate[...] = ds0_ref[...]

    z = z_ref[...].astype(F32)
    sg = sigmoid(z)
    mixed = z * sg
    tok = tok_ref[...]
    tok_bf = tok.astype(BF)
    xc = mixed[:, :inner]
    dt_wide = dot(tok_bf, spread_ref[...])
    xt = (xc * dt_wide).astype(BF)
    b_rows = mixed[:, inner : inner + STATE].astype(BF)
    c_rows = mixed[:, inner + STATE :].astype(BF)
    ent = dot(tok_bf, spread_ent_ref[...])
    leave = dot(tok_bf, spread_leave_ref[...])
    dy = dy_ref[...]
    sin = sin_ref[0]
    ds = dstate[...]
    ds_bf = ds.astype(BF)
    dye = dy.astype(F32) * ent
    tokg = dot((dye * dot(c_rows, sin)).astype(BF), gather_ref[1])
    dye = dye.astype(BF)
    dc = dot_tt(dye, sin)
    xt_f = xt.astype(F32)
    dx_state = dot(b_rows, ds_bf) * leave
    dxt[...] = dx_state
    tokg = tokg + dot((xt_f * dx_state).astype(BF), gather_ref[2])
    db = dot_tt((xt_f * leave).astype(BF), ds_bf)
    carry_ref[0] = jnp.sum(ds * sin.astype(F32), axis=0, keepdims=True)
    dstate[...] = ds * decay_ref[0] + dot_00(c_rows, dye)
    mask = linked_mask(seg_ref[...], segrow_ref[...])
    cross = jnp.where(mask, dot_tt(c_rows, b_rows), 0.0)
    later = lax.broadcasted_iota(jnp.int32, (CHUNK, CHUNK), 0)
    earlier = lax.broadcasted_iota(jnp.int32, (CHUNK, CHUNK), 1)
    before = (later < earlier).astype(BF)
    upto = (later >= earlier).astype(F32)
    cum_rows = cum_ref[...]
    dcross = jnp.zeros((CHUNK, CHUNK), F32)
    for j in range(heads // 2):
        at = slice(j * pair_width, (j + 1) * pair_width)
        xp = xt[:, at]
        dys = two_heads(dy[:, at])
        lefts = []
        for i in (0, 1):
            head = 2 * j + i
            decay = decay_pair(tok, cum_rows, head, heads)
            lefts.append((cross * decay).astype(BF))
            w = dot_tt(dys[i], xp) * decay
            dcross = dcross + w
            spans = dot((w * cross).astype(BF), before)
            inlog_ref[head : head + 1, :] = jnp.sum(spans * upto, axis=0, keepdims=True)
        dxt[:, at] += dot_00(jnp.concatenate(lefts, axis=0), jnp.concatenate(dys, axis=0))
    dcross = jnp.where(mask, dcross, 0.0).astype(BF)
    dc = dc + dot(dcross, b_rows)
    db = db + dot_00(dcross, c_rows)
    dx = dxt[...]
    tokg_ref[...] = tokg + dot((xc * dx).astype(BF), gather_ref[0])
    slope = sg * (1.0 + z * (1.0 - sg))
    dz_ref[:, :inner] = ((dx * dt_wide + skip_ref[...] * dy.astype(F32)) * slope[:, :inner]).astype(BF)
    dz_ref[:, inner : inner + STATE] = (db * slope[:, inner : inner + STATE]).astype(BF)
    dz_ref[:, inner + STATE :] = (dc * slope[:, inner + STATE :]).astype(BF)


def gather_rows(shard):
    return lax.all_gather(shard, "wsh", axis=0, tiled=True)


def reduce_rows(term):
    part = lax.psum_scatter(term, "wsh", scatter_dimension=0, tiled=True)
    return lax.psum(part, "seq").astype(F32)


def on_device(
    x_in, seg_ids, g_norm, w_in, conv_w, conv_b, dt_bias, a_log, d_skip, g_gate, w_out, cotangent
):
    seqs = lax.axis_size("seq")
    me = lax.axis_index("seq")
    toks = x_in.shape[1]
    width = x_in.shape[2]
    inner = g_gate.shape[0]
    heads = dt_bias.shape[0]
    head_width = inner // heads
    conv_width = conv_w.shape[1]
    taps = conv_w.shape[0]
    chunks = toks // CHUNK
    sds = jax.ShapeDtypeStruct

    wx = gather_rows(w_in[:, inner:])
    wg = gather_rows(w_in[:, :inner])
    wo = gather_rows(w_out)

    up = [(i, i + 1) for i in range(seqs - 1)]
    down = [(i + 1, i) for i in range(seqs - 1)]
    halo = lax.ppermute(x_in[0, toks - HALO :], "seq", up)
    x_ext = jnp.concatenate([halo, x_in[0]], axis=0).astype(F32)
    r_ext = lax.rsqrt(jnp.mean(x_ext * x_ext, axis=1, keepdims=True) + EPSILON)
    normed_ext = (x_ext * r_ext * g_norm[None, :]).astype(BF)
    normed = normed_ext[HALO:]
    proj = dot(normed_ext, wx).astype(BF)
    gate = dot(normed, wg).astype(BF)
    cot = cotangent[0]
    back = dot_tt(cot, wo).astype(BF)

    start = me * toks
    seg_pad = jnp.concatenate([jnp.full((HALO,), -1, jnp.int32), seg_ids[0], jnp.full((8,), -2, jnp.int32)])
    near = lax.dynamic_slice_in_dim(seg_pad, start, toks + HALO + 8, 0)
    seg = near[HALO : HALO + toks]
    keep = jnp.stack([(near[HALO - k : HALO - k + toks] == seg) for k in range(taps)], axis=1).astype(F32)
    ext_seg = near[: toks + HALO]
    place = jnp.arange(toks + HALO)
    keep_next = jnp.stack(
        [(near[k : k + toks + HALO] == ext_seg) & (place + k < toks + HALO) for k in range(taps)], axis=1
    ).astype(F32)
    seg_before = near[HALO - 1]
    seg_f = seg.astype(F32)
    seg_chunk = seg.reshape(chunks, CHUNK)
    last_chunk = seg_chunk[:, -1]
    prev_chunk = jnp.concatenate([seg_before[None], last_chunk[:-1]])

    step_raw = proj[HALO:, conv_width:].astype(F32) + dt_bias[None, :]
    dt = jax.nn.softplus(step_raw)
    rates = -jnp.exp(a_log)
    logs = (dt * rates[None, :]).reshape(chunks, CHUNK, heads)
    tri = jnp.tril(jnp.ones((CHUNK, CHUNK), F32))
    cum = jnp.einsum("ts,csh->cth", tri, logs, precision=EXACT)
    last = cum[:, -1]
    before = jnp.einsum("cd,dh->ch", jnp.tril(jnp.ones((chunks, chunks), F32), -1), last, precision=EXACT)
    after = jnp.einsum("cd,dh->ch", jnp.triu(jnp.ones((chunks, chunks), F32), 1), last, precision=EXACT)
    total_log = jnp.sum(last, axis=0)
    enter = jnp.exp(cum) * (seg_chunk == prev_chunk[:, None])[:, :, None]
    leave_log = last[:, None] - cum
    leave = jnp.exp(leave_log) * (seg_chunk == last_chunk[:, None])[:, :, None]
    far_enter = jnp.exp(cum + before[:, None]) * (seg_chunk == seg_before)[:, :, None]
    far_leave = (
        jnp.exp(leave_log + after[:, None]) * (seg_chunk == seg[-1])[:, :, None] * dt.reshape(chunks, CHUNK, heads)
    )
    chunk_decay = jnp.exp(last) * (last_chunk == prev_chunk)[:, None]
    decay_wide = jnp.repeat(chunk_decay, head_width, axis=1)[:, None, :]
    flat = lambda v: v.reshape(toks, heads)
    tok = jnp.concatenate([dt, flat(cum), flat(enter), flat(leave)], axis=1)
    far = jnp.concatenate([flat(far_leave), flat(far_leave), flat(far_enter), flat(far_enter)], axis=1)
    cum_rows = flat(cum).T
    seg_row = seg_f[None, :]
    seg_col = seg_f[:, None]
    lanes = 4 * heads
    owner = jnp.arange(inner)[None, :] // head_width
    slot = jnp.arange(lanes)[:, None]
    spread, spread_ent, spread_leave = [(slot == owner + i * heads).astype(BF) for i in (0, 2, 3)]
    gather = jnp.stack([(slot == owner + i * heads).astype(BF).T for i in (0, 1, 2)])
    skip_wide = jnp.repeat(d_skip, head_width)[None, :]

    block = 256
    z = pl.pallas_call(
        conv_kernel,
        grid=(conv_width // block,),
        in_specs=[
            pl.BlockSpec((toks + HALO, block), lambda i: (0, i)),
            pl.BlockSpec((toks, taps), lambda i: (0, 0)),
            pl.BlockSpec((taps, block), lambda i: (0, i)),
            pl.BlockSpec((1, block), lambda i: (0, i)),
        ],
        out_specs=pl.BlockSpec((toks, block), lambda i: (0, i)),
        out_shape=sds((toks, conv_width), BF),
        scratch_shapes=[pltpu.VMEM((toks + HALO, block), F32)],
        compiler_params=params(),
        name="conv",
    )(proj, keep, conv_w, conv_b[None, :])

    rows = lambda n: pl.BlockSpec((CHUNK, n), lambda i: (i, 0))
    whole = lambda a, b: pl.BlockSpec((a, b), lambda i: (0, 0))
    own_state = pl.pallas_call(
        state_kernel,
        grid=(chunks,),
        in_specs=[rows(conv_width), rows(lanes), whole(lanes, inner)],
        out_specs=whole(STATE, inner),
        out_shape=sds((STATE, inner), F32),
        compiler_params=params(),
        name="own_state",
    )(z, far, spread)

    logs_all = lax.all_gather(total_log, "seq", axis=0)
    ids = jnp.arange(seqs)
    ends = seg_ids[0].reshape(seqs, toks)[:, -1]
    starts_before = jnp.concatenate([jnp.full((1,), -1, jnp.int32), ends[:-1]])
    between = (ids[None, :] > jnp.minimum(ids, me)[:, None]) & (ids[None, :] < jnp.maximum(ids, me)[:, None])
    gap = jnp.exp(jnp.sum(jnp.where(between[:, :, None], logs_all[None], 0.0), axis=1))
    from_past = gap * ((ids < me) & (ends == seg_before))[:, None]
    from_next = gap * ((ids > me) & (starts_before == seg[-1]))[:, None]

    def combine(own, weights):
        every = lax.all_gather(own.astype(BF), "seq", axis=0)
        wide = jnp.repeat(weights, head_width, axis=1)[:, None, :]
        return jnp.sum(every.astype(F32) * wide, axis=0)

    y_inside = pl.pallas_call(
        partial(inside_kernel, heads),
        grid=(chunks,),
        in_specs=[
            rows(conv_width), rows(lanes), rows(1),
            pl.BlockSpec((heads, CHUNK), lambda i: (0, i)),
            pl.BlockSpec((1, CHUNK), lambda i: (0, i)),
            whole(lanes, inner), whole(1, inner),
        ],
        out_specs=rows(inner),
        out_shape=sds((toks, inner), BF),
        compiler_params=params(),
        name="inside",
    )(z, tok, seg_col, cum_rows, seg_row, spread, skip_wide)
    first_state = combine(own_state, from_past)

    states, gated_out, dgate, dy, dgain, dskip_wide, own_ds = pl.pallas_call(
        gate_kernel,
        grid=(chunks,),
        in_specs=[
            rows(inner), rows(conv_width), rows(inner), rows(inner), rows(lanes), rows(lanes),
            pl.BlockSpec((1, 1, inner), lambda i: (i, 0, 0)),
            whole(1, inner), whole(STATE, inner),
            whole(lanes, inner), whole(lanes, inner), whole(lanes, inner),
        ],
        out_specs=[
            pl.BlockSpec((1, STATE, inner), lambda i: (i, 0, 0)),
            rows(inner), rows(inner), rows(inner),
            whole(1, inner), whole(1, inner), whole(STATE, inner),
        ],
        out_shape=[
            sds((chunks, STATE, inner), BF),
            sds((toks, inner), BF), sds((toks, inner), BF), sds((toks, inner), BF),
            sds((1, inner), F32), sds((1, inner), F32), sds((STATE, inner), F32),
        ],
        scratch_shapes=[pltpu.VMEM((STATE, inner), F32)],
        compiler_params=params(),
        name="gate",
    )(y_inside, z, gate, back, tok, far, decay_wide, g_gate[None, :], first_state, spread, spread_ent, spread_leave)

    last_ds = combine(own_ds, from_next)
    result = (x_ext[HALO:] + dot(gated_out, wo)).astype(BF)
    w_out_grad = reduce_rows(dot_00(gated_out, cot).astype(BF))
    gate_term = dot_00(normed, dgate).astype(BF)
    gate_rows = reduce_rows(gate_term)

    flip = lambda n: pl.BlockSpec((CHUNK, n), lambda i: (chunks - 1 - i, 0))
    dz, tokg, inlog, carry = pl.pallas_call(
        partial(back_kernel, heads),
        grid=(chunks,),
        in_specs=[
            flip(inner), flip(conv_width), flip(lanes), flip(1),
            pl.BlockSpec((heads, CHUNK), lambda i: (0, chunks - 1 - i)),
            pl.BlockSpec((1, CHUNK), lambda i: (0, chunks - 1 - i)),
            pl.BlockSpec((1, 1, inner), lambda i: (chunks - 1 - i, 0, 0)),
            whole(1, inner),
            pl.BlockSpec((1, STATE, inner), lambda i: (chunks - 1 - i, 0, 0)),
            whole(STATE, inner),
            whole(lanes, inner), whole(lanes, inner), whole(lanes, inner),
            pl.BlockSpec((3, inner, lanes), lambda i: (0, 0, 0)),
        ],
        out_specs=[
            flip(conv_width), flip(lanes),
            pl.BlockSpec((heads, CHUNK), lambda i: (0, chunks - 1 - i)),
            pl.BlockSpec((1, 1, inner), lambda i: (chunks - 1 - i, 0, 0)),
        ],
        out_shape=[
            sds((toks, conv_width), BF), sds((toks, lanes), F32), sds((heads, toks), F32),
            sds((chunks, 1, inner), F32),
        ],
        scratch_shapes=[pltpu.VMEM((STATE, inner), F32), pltpu.VMEM((CHUNK, inner), F32)],
        compiler_params=params(),
        name="scan_back",
    )(
        dy, z, tok, seg_col, cum_rows, seg_row, decay_wide, skip_wide, states, last_ds,
        spread, spread_ent, spread_leave, gather,
    )

    dxbc, dconv_w, dconv_b = pl.pallas_call(
        conv_back_kernel,
        grid=(conv_width // block,),
        in_specs=[
            pl.BlockSpec((toks, block), lambda i: (0, i)),
            pl.BlockSpec((toks + HALO, block), lambda i: (0, i)),
            pl.BlockSpec((toks, taps), lambda i: (0, 0)),
            pl.BlockSpec((toks + HALO, taps), lambda i: (0, 0)),
            pl.BlockSpec((taps, block), lambda i: (0, i)),
        ],
        out_specs=[
            pl.BlockSpec((toks + HALO, block), lambda i: (0, i)),
            pl.BlockSpec((taps, block), lambda i: (0, i)),
            pl.BlockSpec((1, block), lambda i: (0, i)),
        ],
        out_shape=[
            sds((toks + HALO, conv_width), BF), sds((taps, conv_width), F32), sds((1, conv_width), F32),
        ],
        scratch_shapes=[
            pltpu.VMEM((toks + HALO, block), F32), pltpu.VMEM((toks + HALO + 8, block), F32),
        ],
        compiler_params=params(),
        name="conv_back",
    )(dz, proj, keep, keep_next, conv_w)

    tokg = tokg.reshape(chunks, CHUNK, lanes)
    from_dx, from_enter, from_leave = [tokg[:, :, i * heads : (i + 1) * heads] for i in range(3)]
    whole_chunk = jnp.sum(carry.reshape(chunks, heads, head_width), axis=2) * chunk_decay
    dlog = (
        inlog.T.reshape(chunks, CHUNK, heads)
        + jnp.einsum("ut,cth->cuh", tri.T, from_enter, precision=EXACT)
        + jnp.einsum("us,csh->cuh", tri - jnp.eye(CHUNK, dtype=F32), from_leave, precision=EXACT)
        + whole_chunk[:, None, :]
    )
    dlog = flat(dlog)
    drate = jnp.sum(dlog * dt, axis=0)
    dstep = (flat(from_dx) + dlog * rates[None, :]) * jax.nn.sigmoid(step_raw)
    dstep_bf = dstep.astype(BF)

    dproj = jnp.concatenate([dxbc, jnp.pad(dstep_bf, ((HALO, 0), (0, 0)))], axis=1)
    x_rows = reduce_rows(dot_00(normed_ext, dproj).astype(BF))
    w_in_grad = jnp.concatenate([gate_rows, x_rows], axis=1)
    dn_ext = dot_tt(dproj, wx)
    over = lax.ppermute(dn_ext[:HALO], "seq", down)
    dn = dn_ext[HALO:] + dot_tt(dgate, wg)
    dn = dn + jnp.pad(over, ((toks - HALO, 0), (0, 0)))
    x_f = x_ext[HALO:]
    r = r_ext[HALO:]
    f = dn * g_norm[None, :]
    x_grad = cot.astype(F32) + r * f - x_f * (r * r * r) * jnp.mean(f * x_f, axis=1, keepdims=True)
    g_norm_part = jnp.sum(dn * x_f * r, axis=0)

    small = (
        g_norm_part,
        dconv_w,
        dconv_b[0],
        jnp.sum(dstep, axis=0),
        drate * rates,
        jnp.sum(dskip_wide.reshape(heads, head_width), axis=1),
        dgain[0],
    )
    small = lax.psum(small, ("seq", "wsh"))
    return (result[None], x_grad[None], small[0], w_in_grad) + tuple(small[1:]) + (w_out_grad,)


def solution(mesh):
    tokens = P("wsh", "seq", None)
    owned = P("wsh", None)
    return jax.shard_map(
        on_device,
        mesh=mesh,
        in_specs=(tokens, owned, P(), owned, P(), P(), P(), P(), P(), P(), owned, tokens),
        out_specs=(tokens, tokens, P(), owned, P(), P(), P(), P(), P(), P(), owned),
        check_vma=False,
    )
```

time: 3170 us -> 585 us (0.18)
  local copies, waits for them, and re-layouts: 885 us -> 25.1 us
  waiting for transfers between devices: 871 us -> 210 us
  other arithmetic: 607 us -> 52.3 us
  matrix products: 535 us -> 96.1 us
  Pallas kernels: 0 us -> 114 us
  loops' own time: 90.6 us -> 0 us
  blocking collectives: 97.7 us -> 58.8 us
  starting transfers between devices: 37 us -> 4.93 us
    all_to_all x8 -> x0, waiting for transfers between devices: 510 us -> none  [the longest x1 125 us: on_device(): lax.all_to_all(normed_heads, 'seq', split_axis=0, concat_axis=1, tiled=True)]
    dynamic_update_slice x163 -> x0, local copies, waits for them, and re-layouts: 471 us -> none  [the longest x160 470 us: state_scan(): final_carry, outputs = lax.scan(stepper, initial, pieces)]
    dot_general x454 -> x14, matrix products: 535 us -> 96.1 us  [the longest x3 32 us: dot_tt(): lax.dot_general(a, b, (((1,), (1,)), ((), ())), preferred_element_type=F32)]
    another operation x288 -> x2, other arithmetic: 247 us -> 1.53 us  [the longest x1 1.45 us: on_device(): jnp.stack([(slot == owner + i * heads).astype(BF).T for i in (0, 1, 2)])]
    reduce_sum x105 -> x8, other arithmetic: 140 us -> 11.1 us  [the longest x2 8.23 us: combine(): return jnp.sum(every.astype(F32) * wide, axis=0)]
    pallas_call x0 -> x6, Pallas kernels: none -> 114 us  [the longest x1 37.1 us: on_device(): pl.pallas_call(partial(back_kernel, heads), grid=(chunks,), in_specs=[fli...]
    squeeze x128 -> x1, local copies, waits for them, and re-layouts: 93.3 us -> 0.01 us  [on_device(): halo = lax.ppermute(x_in[0, toks - HALO:], 'seq', up)]
    another operation x2 -> x0, loops' own time: 90.6 us -> none  [state_scan(): final_carry, outputs = lax.scan(stepper, initial, pieces)]
  transfers between devices with their start and end apart: 15 -> 11, of which waited for: 9 -> 8; matrix products, arithmetic and copies ran while one was open for 26% -> 27% of each run, Pallas kernels for 0% -> 15%
where the time goes in v1:
time: 585 us; the launch traced here: 577 us
  waiting for transfers between devices  210 us (36%)
  Pallas kernels  114 us (19%)
  matrix products  96.1 us (16%)
  blocking collectives  58.8 us (10%)
  other arithmetic  52.3 us (9%)
  local copies, waits for them, and re-layouts  25.1 us (4%)
  between operations  15.3 us (3%)
    all_gather x3, waiting for transfers between devices, gather_rows(): return lax.all_gather(shard, 'wsh', axis=0, tiled=True)  96 us
    reduce_scatter x3, waiting for transfers between devices, reduce_rows(): part = lax.psum_scatter(term, 'wsh', scatter_dimension=0, tiled=True)  65 us
    psum x1, blocking collectives, on_device(): small = lax.psum(small, ('seq', 'wsh'))  41.8 us
    pallas_call x1, Pallas kernels, on_device(): pl.pallas_call(partial(back_kernel, heads), grid=(chunks,), in_specs=[fli...  37.1 us
    dot_general x3, matrix products, dot_tt(): lax.dot_general(a, b, (((1,), (1,)), ((), ())), preferred_element_type=F32)  32 us
    dot_general x3, matrix products, dot_00(): lax.dot_general(a, b, (((0,), (0,)), ((), ())), preferred_element_type=F32)  29.8 us
    dot_general x3, matrix products, dot(): return jnp.dot(a, b, preferred_element_type=F32)  28.6 us
    pallas_call x1, Pallas kernels, on_device(): pl.pallas_call(gate_kernel, grid=(chunks,), in_specs=[rows(inner), rows(c...  25.8 us
  transfers between devices with their start and end apart: 11, of which 8 were waited for; matrix products, arithmetic and copies ran while one was open for 27% of the time, Pallas kernels for 15%

profile of v1, /device:TPU:0, one launch (start us, length us, event | category | flops | bytes accessed | tf_op | source)
XLA Modules:
  0.0 576.7 jit_solution(10985128411616593425)
XLA Ops:
  7.3 2.5 slice.99
  9.9 2.3 slice.112
  12.2 2.4 collective-permute-start
  23.6 1.9 multiply_convert_fusion
  25.4 45.2 %all-gather.9.cloned.1.call-done = bf16[1024,2336]{0,1:T(8,128)(2,1)} async-done(((bf16[256,2336]{0,1:T(8,128)(2,1)}), bf16[1024,2336]{0,1:T(8,128)(2,1)}) %all-gather.9.cloned.1.call-update) | async-done | bytes 4784144 | tf_op jit(solution)/shard_map/all_gather | solution.py:254
  70.7 8.6 %convolution_convert_fusion.x_ref = bf16[1040,2336]{1,0:T(8,128)(2,1)S(1)} fusion(bf16[1040,1024]{1,0:T(8,128)(2,1)} %multiply_convert_fusion, bf16[1024,2336]{0,1:T(8,128)(2,1)} %all-gather.9.cloned.1.call-done), kind=kOutput, calls=%fused_computation | convolution fusion | flops 4977922560 | bytes 11772928 | tf_op jit(solution)/shard_map/dot_general | solution.py:21
  79.3 2.2 copy-done
  84.0 2.4 copy_multiply_fusion
  86.6 11.7 %conv.1.z_ref = bf16[1024,2304]{1,0:T(8,128)(2,1)} custom-call(bf16[1040,2336]{1,0:T(8,128)(2,1)} %copy-done, f32[1024,4]{1,0:T(8,128)} %convert_element_type.148.keep_ref, f32[4,2304]{1,0:T(4,128)} %w_ref.3, f32[1,2304]{1,0:T(1,128)} %broadcast_in_dim.52.b_ref), custom_call_target="tpu_custom_call" | custom-call | tf_op jit(solution)/shard_map/conv/pallas_call | solution.py:342
  99.6 9.1 %own_state.1 = f32[128,2048]{1,0:T(8,128)} custom-call(bf16[1024,2304]{1,0:T(8,128)(2,1)} %conv.1.z_ref, f32[1024,128]{1,0:T(8,128)} %pad_maximum_fusion.1.tok_ref.far_ref, bf16[128,2048]{1,0:T(8,128)(2,1)} %fusion.16.spread_ref), custom_call_target="tpu_custom_call" | custom-call | tf_op jit(solution)/shard_map/own_state/pallas_call | solution.py:360
  108.7 2.1 convert_element_type.158
  116.9 1.3 convert_reduce_fusion
  120.1 5.5 all-gather.11.cloned.1.call-done
  125.7 9.4 %convolution_convert_fusion.5.gate_ref = bf16[1024,2048]{1,0:T(8,128)(2,1)} fusion(bf16[1024,2048]{0,1:T(8,128)(2,1)} %all-gather.11.cloned.1.call-done, bf16[1040,1024]{1,0:T(8,128)(2,1)} %multiply_convert_fusion), kind=kOutput, calls=%fused_computation.20 | convolution fusion | flops 4297064448 | bytes 10485760 | tf_op jit(solution)/shard_map/dot_general | solution.py:21
  135.0 45.2 %all-gather.13.cloned.1.call-done = bf16[2048,1024]{1,0:T(8,128)(2,1)} async-done(((bf16[512,1024]{1,0:T(8,128)(2,1)}), bf16[2048,1024]{1,0:T(8,128)(2,1)}) %all-gather.13.cloned.1.call-update) | async-done | bytes 4194320 | tf_op jit(solution)/shard_map/all_gather | solution.py:254
  180.3 9.3 %convolution_convert_fusion.4.back_ref = bf16[1024,2048]{1,0:T(8,128)(2,1)} fusion(bf16[2048,1024]{1,0:T(8,128)(2,1)} %all-gather.13.cloned.1.call-done, bf16[1,1024,1024]{2,1,0:T(8,128)(2,1)} %param.23), kind=kOutput, calls=%fused_computation.19 | convolution fusion | flops 4297064448 | bytes 10485760 | tf_op jit(solution)/shard_map/dot_general | solution.py:25
  189.8 17.1 %all-reduce.2 = f32[256]{0:T(256)S(1)} all-reduce(f32[256]{0:T(256)S(1)} %dynamic-update-slice), channel_id=3, replica_groups=mesh['seq'=8,'wsh'=4] {'seq'}, use_global_device_ids=true, to_apply=%add.2 | all-reduce | flops 256 | bytes 2048
  207.3 1.9 copy.144
  212.8 2.5 pad_maximum_fusion.tok_ref
  215.3 12.0 %inside.1.yi_ref = bf16[1024,2048]{1,0:T(8,128)(2,1)} custom-call(bf16[1024,2304]{1,0:T(8,128)(2,1)} %conv.1.z_ref, f32[1024,128]{1,0:T(8,128)} %pad_maximum_fusion.tok_ref, f32[1024,1]{1,0:T(8,128)} %copy.145.seg_ref, f32[32,1024]{1,0:T(8,128)} %copy.146.cum_ref, f32[1,1024]{1,0:T(1,128)} %bitcast.137, bf16[128,2048]{1,0:T(8,128)(2,1)} %fusion.16.spread_ref, ...), custom_call_target="tpu_custom_call" | custom-call | tf_op jit(solution)/shard_map/inside/pallas_call | solution.py:384
  227.3 1.9 all-gather.15.cloned.1.call-done
  229.2 4.1 fusion.2.s0_ref
  233.3 25.8 %gate.1 = (bf16[8,128,2048]{2,1,0:T(8,128)(2,1)}, bf16[1024,2048]{1,0:T(8,128)(2,1)}, bf16[1024,2048]{1,0:T(8,128)(2,1)}, bf16[1024,2048]{1,0:T(8,128)(2,1)}, f3...) custom-call(bf16[1024,2048]{1,0:T(8,128)(2,1)} %inside.1.yi_ref, bf16[1024,2304]{1,0:T(8,128)(2,1)} %conv.1.z_ref, ...), custom_call_target="tpu_custom_call" | custom-call | tf_op jit(solution)/shard_map/gate/pallas_call | solution.py:400
  259.1 2.1 convert_element_type.164
  261.3 9.4 %convolution_convert_fusion.3 = bf16[1024,2048]{1,0:T(8,128)(2,1)} fusion(bf16[1024,2048]{1,0:T(8,128)(2,1)} %get-tuple-element.34, bf16[1040,1024]{1,0:T(8,128)(2,1)} %multiply_convert_fusion), kind=kOutput, calls=%fused_computation.18 | convolution fusion | flops 4297064448 | bytes 10485760 | tf_op jit(solution)/shard_map/dot_general | solution.py:29
  270.8 9.4 %convolution_convert_fusion.2 = bf16[2048,1024]{1,0:T(8,128)(2,1)} fusion(bf16[1024,2048]{1,0:T(8,128)(2,1)} %get-tuple-element.25, bf16[1,1024,1024]{2,1,0:T(8,128)(2,1)} %param.23), kind=kOutput, calls=%fused_computation.17 | convolution fusion | flops 4297064448 | bytes 10485760 | tf_op jit(solution)/shard_map/dot_general | solution.py:29
  283.3 1.4 add_convert_fusion.1.gather_ref
  285.0 22.3 %all-gather.17.cloned.1.call-done = bf16[1024,2048]{1,0:T(8,128)(2,1)} async-done(((bf16[128,2048]{1,0:T(8,128)(2,1)}), bf16[1024,2048]{1,0:T(8,128)(2,1)}) %all-gather.17.cloned.1.call-update) | async-done | bytes 4194320 | tf_op jit(solution)/shard_map/all_gather | solution.py:380
  307.2 4.1 fusion.1.ds0_ref
  311.3 37.1 %scan_back.1 = (bf16[1024,2304]{1,0:T(8,128)(2,1)}, f32[1024,128]{1,0:T(8,128)}, f32[32,1024]{1,0:T(8,128)}, f32[8,1,2048]{2,1,0:T(1,128)}) custom-call(bf16[1024,2048]{1,0:T(8,128)(2,1)} %get-tuple-element.26.dy_ref, bf16[1024,2304]{1,0:T(8,128)(2,1)} %conv.1.z_ref, f32[1024,128]{1,0:T(8,128)} %pad_maximum_fusion.tok_ref, f32[1024,1]{1,0:T(8,128)} %copy.145.seg_ref, ...), custom_call_target="tpu_custom_call" | custom-call | tf_op jit(solution)/shard_map/scan_back/pallas_call | solution.py:431
  350.4 2.2 fusion.15
  352.6 2.2 fusion.14
  355.1 18.7 %conv_back.1 = (bf16[1040,2304]{1,0:T(8,128)(2,1)}, f32[4,2304]{1,0:T(4,128)}, f32[1,2304]{1,0:T(1,128)}) custom-call(bf16[1024,2304]{1,0:T(8,128)(2,1)} %get-tuple-element.29.dz_ref, bf16[1040,2336]{1,0:T(8,128)(2,1)} %copy-done, f32[1024,4]{1,0:T(8,128)} %convert_element_type.148.keep_ref, f32[1040,4]{1,0:T(8,128)} %copy.156.next_ref, f32[4,2304]{1,0:T(4,128)} %w_ref.3), custom_call_target="tpu_custom_call" | custom-call | tf_op jit(solution)/shard_map/conv_back/pallas_call | solution.py:462
  373.8 1.5 fusion.69
  375.3 11.0 %convolution_convert_fusion.1 = bf16[1024,2336]{0,1:T(8,128)(2,1)} fusion(bf16[1040,1024]{1,0:T(8,128)(2,1)S(1)} %copy-done.4, bf16[1024,32]{1,0:T(8,128)(2,1)S(1)} %get-tuple-element.52, bf16[1040,2304]{1,0:T(8,128)(2,1)} %get-tuple-element.30), kind=kOutput, calls=%fused_computation.7 | convolution fusion | flops 4992461824 | bytes 11771904 | tf_op jit(solution)/shard_map/dot_general | solution.py:29
  387.1 2.5 maximum_convert_fusion.1
  391.0 10.6 %fusion.5 = bf16[1,1024,1024]{2,1,0:T(8,128)(2,1)} fusion(f32[1040,1024]{1,0:T(8,128)} %maximum_convert_fusion.1, bf16[1024,2048]{1,0:T(8,128)(2,1)} %get-tuple-element.25, bf16[2048,1024]{1,0:T(8,128)(2,1)} %all-gather.13.cloned.1.call-done), kind=kOutput, calls=%fused_computation.24 | convolution fusion | flops 4297064448 | bytes 14680064 | tf_op jit(solution)/shard_map/dot_general | solution.py:21
  401.6 9.9 %fusion.9 = f32[1040,1024]{1,0:T(8,128)S(1)} fusion(bf16[1024,2336]{0,1:T(8,128)(2,1)} %all-gather.9.cloned.1.call-done, bf16[1024,32]{1,0:T(8,128)(2,1)S(1)} %get-tuple-element.52, bf16[1040,2304]{1,0:T(8,128)(2,1)} %get-tuple-element.30), kind=kOutput, calls=%fused_computation.27 | convolution fusion | flops 4990069760 | bytes 13901824 | tf_op jit(solution)/shard_map/dot_general | solution.py:25
  411.5 1.5 collective-permute-start.1
  413.6 4.4 reduce-scatter.8.cloned.1.call-done
  418.0 60.6 %reduce-scatter.6.cloned.1.call-done = bf16[256,2336]{0,1:T(8,128)(2,1)} async-done(((bf16[1024,2336]{0,1:T(8,128)(2,1)}), bf16[256,2336]{0,1:T(8,128)(2,1)}) %reduce-scatter.6.cloned.1.call-update) | async-done | bytes 1196048 | tf_op jit(solution)/shard_map/reduce_scatter | solution.py:258
  478.7 12.8 %multiply_reduce_fusion.1 = (f32[1024]{0:T(1024)S(1)}, f32[1024]{0:T(1024)S(1)}, f32[1024,1024]{1,0:T(8,128)}) fusion(f32[1040,1024]{1,0:T(8,128)} %maximum_convert_fusion.1, f32[1024]{0:T(1024)S(1)} %slice.132, f32[1024]{0:T(1024)S(1)} %copy-done.17, f32[16,1024]{1,0:T(8,128)S(1)} %collective-permute-done.1, bf16[1024,2048]{1,0:T(8,128)(2,1)} %get-tuple-element.34, ...), kind=kOutput, calls=%fused_computation.13 | convolution fusion | flops 4303353856 | bytes 21053440 | tf_op jit(solution)/shard_map/dot_general | solution.py:25
  491.6 41.8 %all-reduce.3 = (f32[1024]{0:T(1024)}, f32[4,2304]{1,0:T(4,128)}, f32[2304]{0:T(1024)}, f32[32]{0:T(128)}, f32[32]{0:T(128)}, /*index=5*/f32[32]{0:T(128)}, f32[2048]{0:T(1024)}) all-reduce(f32[1024]{0:T(1024)S(1)} %get-tuple-element.39, f32[4,2304]{1,0:T(4,128)S(1)} %copy-done.15, ...), channel_id=1, replica_groups=mesh['seq'=8,'wsh'=4] {'seq','wsh'}, use_global_device_ids=true, to_apply=%region_8.9 | all-reduce | flops 14688 | bytes 117504 | tf_op jit(solution)/shard_map/psum | solution.py:523
  533.3 5.5 subtract_bitcast_fusion
  538.8 24.4 %all-reduce.7.cloned.1.call-done = (bf16[256,2336]{0,1:T(8,128)(2,1)}, bf16[256,2048]{1,0:T(8,128)(2,1)}, bf16[512,1024]{1,0:T(8,128)(2,1)}) async-done(((bf16[256,2336]{0,1:T(8,128)(2,1)}, bf16[256,2048]{1,0:T(8,128)(2,1)}, bf16[512,1024]{1,0:T(8,128)(2,1)}), (bf16[256,2336]{0,1:T(8,128)(2,1)}, bf16[256,2048]{1,0:T(8,128)(2,1)}, bf16[512,1024]{1,0:T(8,128)(2,1)})) %all-reduce.7.cloned.1.call-update) | async-done | bytes 3293200 | tf_op jit(solution)/shard_map/psum | solution.py:259
  563.2 1.6 copy.161
  564.8 2.8 convert_element_type.173
  567.6 2.5 maximum_convert_fusion
  (185 shorter events, 32.8 us)
Async XLA Ops:
  7.2 5.0 copy-start.1
  7.2 7.5 %copy-start.8 = (s32[1,8192]{1,0:T(1,128)S(1)}, s32[1,8192]{1,0:T(1,128)}, u32[]{:S(2)}) copy-start(s32[1,8192]{1,0:T(1,128)} %param.13) | copy-start | bytes 98308
  7.2 10.7 %copy-start.31 = (f32[32]{0:T(128)S(1)}, f32[32]{0:T(128)}, u32[]{:S(2)}) copy-start(f32[32]{0:T(128)} %param.19) | copy-start | bytes 388
  7.2 63.4 %all-gather.9.cloned.1.call-start = ((), (), s32[]{:S(2)}) async-start(), calls=%async_computation.3 | async-start | bytes 5980160 | tf_op jit(solution)/shard_map/all_gather | solution.py:254
  9.8 12.1 %copy-start.19 = (f32[2304]{0:T(1024)S(1)}, f32[2304]{0:T(1024)}, u32[]{:S(2)}) copy-start(f32[2304]{0:T(1024)} %param.17) | copy-start | bytes 27652
  9.8 13.8 %copy-start.16 = (f32[1024]{0:T(1024)S(1)}, f32[1024]{0:T(1024)}, u32[]{:S(2)}) copy-start(f32[1024]{0:T(1024)} %param.14) | copy-start | bytes 12292
  9.8 115.9 %all-gather.11.cloned.1.call-start = ((), (), s32[]{:S(2)}) async-start(), calls=%async_computation.4 | async-start | bytes 5242880 | tf_op jit(solution)/shard_map/all_gather | solution.py:254
  12.1 168.1 %all-gather.13.cloned.1.call-start = ((), (), s32[]{:S(2)}) async-start(), calls=%async_computation.5 | async-start | bytes 5242880 | tf_op jit(solution)/shard_map/all_gather | solution.py:254
  12.2 10.2 %collective-permute-start = (bf16[16,1024]{1,0:T(8,128)(2,1)S(1)}, bf16[16,1024]{1,0:T(8,128)(2,1)S(1)}, u32[]{:S(2)}, u32[]{:S(2)}) collective-permute-start(bf16[16,1024]{1,0:T(8,128)(2,1)S(1)} %slice_bitcast_fusion), channel_id=1, source_target_pairs={{0,4},{4,8},{8,12},{12,16},{16,20},{20,24},{24,28},{1,5},{5,9},{9,... | collective-permute-start | bytes 98312 | tf_op jit(solution)/shard_map/ppermute | solution.py:283
  14.6 214.6 %all-gather.15.cloned.1.call-start = ((), (), s32[]{:S(2)}) async-start(), calls=%async_computation.9 | async-start | bytes 4718592 | tf_op jit(solution)/shard_map/all_gather | solution.py:380
  18.0 1.9 copy-start.10
  18.0 61.3 %copy-start.26 = (f32[32]{0:T(128)}, f32[32]{0:T(128)S(1)}, u32[]{:S(2)}) copy-start(f32[32]{0:T(128)S(1)} %exponential_negate_fusion) | copy-start | bytes 388
  23.0 0.6 copy-start.13
  25.4 56.1 %copy-start.24 = (f32[32]{0:T(128)S(1)}, f32[32]{0:T(128)}, u32[]{:S(2)}) copy-start(f32[32]{0:T(128)} %param.18) | copy-start | bytes 388
  79.3 2.2 copy-start
  83.1 15.2 %copy-start.3 = (f32[8,32,128]{1,0,2:T(8,128)}, f32[8,32,128]{1,0,2:T(8,128)S(1)}, u32[]{:S(2)}) copy-start(f32[8,32,128]{1,0,2:T(8,128)S(1)} %copy.139) | copy-start | bytes 393220
  99.6 12.3 %copy-start.9 = (s32[1,8192]{1,0:T(1,128)S(1)}, s32[1,8192]{1,0:T(1,128)}, u32[]{:S(2)}) copy-start(s32[1,8192]{1,0:T(1,128)} %param.13) | copy-start | bytes 98308
  99.6 14.5 %copy-start.29 = (f32[32]{0:T(128)S(1)}, f32[32]{0:T(128)}, u32[]{:S(2)}) copy-start(f32[32]{0:T(128)} %param.20) | copy-start | bytes 388
  99.6 15.3 %copy-start.33 = (u32[32]{0:T(128)S(1)}, u32[32]{0:T(128)}, u32[]{:S(2)}) copy-start(u32[32]{0:T(128)} %constant.93) | copy-start | bytes 388
  99.6 17.2 %copy-start.18 = (s32[7,1]{1,0:T(8,128)S(1)}, s32[7,1]{1,0:T(8,128)}, u32[]{:S(2)}) copy-start(s32[7,1]{1,0:T(8,128)} %get-tuple-element.74) | copy-start | bytes 88
  110.8 196.4 %all-gather.17.cloned.1.call-start = ((), (), s32[]{:S(2)}) async-start(), calls=%async_computation.10 | async-start | bytes 4718592 | tf_op jit(solution)/shard_map/all_gather | solution.py:380
  113.1 22.0 %copy-start.12 = (f32[1024]{0:T(1024)}, f32[1024]{0:T(1024)S(1)}, u32[]{:S(2)}) copy-start(f32[1024]{0:T(1024)S(1)} %dynamic-slice_convert_fusion) | copy-start | bytes 12292
  135.0 54.6 %copy-start.30 = (f32[32]{0:T(128)S(1)}, f32[32]{0:T(128)}, u32[]{:S(2)}) copy-start(f32[32]{0:T(128)} %get-tuple-element.60) | copy-start | bytes 388
  135.0 74.2 %copy-start.5 = (f32[8,128,32]{2,0,1:T(8,128)S(1)}, f32[8,128,32]{2,0,1:T(8,128)}, u32[]{:S(2)}) copy-start(f32[8,128,32]{2,0,1:T(8,128)} %get-tuple-element.63) | copy-start | bytes 393220
  261.3 152.4 %reduce-scatter.4.cloned.1.call-start = ((), (), s32[]{:S(2)}) async-start(), calls=%async_computation.6 | async-start | bytes 5242880 | tf_op jit(solution)/shard_map/reduce_scatter | solution.py:258
  270.7 147.3 %reduce-scatter.8.cloned.1.call-start = ((), (), s32[]{:S(2)}) async-start(), calls=%async_computation.8 | async-start | bytes 5242880 | tf_op jit(solution)/shard_map/reduce_scatter | solution.py:258
  280.2 1.5 copy-start.11
  280.2 198.4 %reduce-scatter.6.cloned.1.call-start = ((), (), s32[]{:S(2)}) async-start(), calls=%async_computation.7 | async-start | bytes 5980160 | tf_op jit(solution)/shard_map/reduce_scatter | solution.py:258
  311.3 38.3 %copy-start.23 = (f32[8]{0:T(128)S(1)}, f32[8]{0:T(128)}, u32[]{:S(2)}) copy-start(f32[8]{0:T(128)} %convert_reduce_fusion) | copy-start | bytes 100
  355.0 18.8 %copy-start.2 = (f32[1024,128]{1,0:T(8,128)S(1)}, f32[1024,128]{1,0:T(8,128)}, u32[]{:S(2)}) copy-start(f32[1024,128]{1,0:T(8,128)} %get-tuple-element.31) | copy-start | bytes 1572868
  355.0 18.8 %copy-start.25 = (f32[32]{0:T(128)S(1)}, f32[32]{0:T(128)}, u32[]{:S(2)}) copy-start(f32[32]{0:T(128)} %param.18) | copy-start | bytes 388
  355.0 18.8 %copy-start.27 = (f32[32]{0:T(128)S(1)}, f32[32]{0:T(128)}, u32[]{:S(2)}) copy-start(f32[32]{0:T(128)} %copy-done.26) | copy-start | bytes 388
  355.0 20.3 %copy-start.4 = (bf16[1040,1024]{1,0:T(8,128)(2,1)S(1)}, bf16[1040,1024]{1,0:T(8,128)(2,1)}, u32[]{:S(2)}) copy-start(bf16[1040,1024]{1,0:T(8,128)(2,1)} %multiply_convert_fusion) | copy-start | bytes 6389764
  386.3 0.7 copy-start.14
  386.3 3.8 copy-start.22
  386.3 176.8 %all-reduce.7.cloned.1.call-start = ((), (), s32[]{:S(2)}) async-start(), calls=%async_computation.11 | async-start | bytes 6586368 | tf_op jit(solution)/shard_map/psum | solution.py:259
  401.6 11.4 %copy-start.32 = (f32[32]{0:T(128)S(1)}, f32[32]{0:T(128)}, u32[]{:S(2)}) copy-start(f32[32]{0:T(128)} %param.19) | copy-start | bytes 388
  401.6 12.0 %copy-start.20 = (f32[1,2304]{1,0:T(1,128)S(1)}, f32[1,2304]{1,0:T(1,128)}, u32[]{:S(2)}) copy-start(f32[1,2304]{1,0:T(1,128)} %get-tuple-element.36) | copy-start | bytes 27652
  401.6 77.1 %copy-start.17 = (f32[1024]{0:T(1024)S(1)}, f32[1024]{0:T(1024)}, u32[]{:S(2)}) copy-start(f32[1024]{0:T(1024)} %param.14) | copy-start | bytes 12292
  411.5 2.1 copy-start.28
  411.5 67.2 %collective-permute-start.1 = (f32[16,1024]{1,0:T(8,128)S(1)}, f32[16,1024]{1,0:T(8,128)S(1)}, u32[]{:S(2)}, u32[]{:S(2)}) collective-permute-start(f32[16,1024]{1,0:T(8,128)S(1)} %slice.138), channel_id=1, source_target_pairs={{4,0},{8,4},{12,8},{16,12},{20,16},{24,20},{28,24},{5,1},{9,5},{13... | collective-permute-start | bytes 196616 | tf_op jit(solution)/shard_map/ppermute | solution.py:505
  478.7 12.9 %copy-start.15 = (f32[4,2304]{1,0:T(4,128)S(1)}, f32[4,2304]{1,0:T(4,128)}, u32[]{:S(2)}) copy-start(f32[4,2304]{1,0:T(4,128)} %get-tuple-element.35) | copy-start | bytes 110596
  478.7 12.9 %copy-start.21 = (f32[1,2048]{1,0:T(1,128)S(1)}, f32[1,2048]{1,0:T(1,128)}, u32[]{:S(2)}) copy-start(f32[1,2048]{1,0:T(1,128)} %get-tuple-element.38) | copy-start | bytes 24580
  478.7 54.6 %copy-start.6 = (bf16[1,1024,1024]{2,1,0:T(8,128)(2,1)S(1)}, bf16[1,1024,1024]{2,1,0:T(8,128)(2,1)}, u32[]{:S(2)}) copy-start(bf16[1,1024,1024]{2,1,0:T(8,128)(2,1)} %param.23) | copy-start | bytes 6291460
  563.2 4.4 copy-start.7
Sparse Core Ops, SparseCore 0:
  10.4 60.1 all-gather.8
  73.0 52.5 all-gather.10
  127.5 52.6 all-gather.12
  181.7 47.4 all-gather.14
  261.4 45.8 all-gather.16
  310.6 51.4 reduce-scatter.3
  365.3 52.6 reduce-scatter.7
  421.0 57.5 reduce-scatter.5
  481.3 81.8 all-reduce.6
